TPU v7x, 32 devices: a whole 2x2x4 slice. The times are simulated.
32 devices in a mesh: sib: 2 (over y), row: 4 (over z), col: 4 (over x, core).
Axes of the slice: x: 2, y: 2, z: 4, core: 2. Of those that a mesh axis runs over, the one named last changes fastest.
Arguments:
- eigvec: bfloat16 [2, 4096, 8192], P('sib', 'row', 'col'), may hold values from -6 to 6
- poles: float32 [2, 8192], P('sib', 'col'), may hold values from 0 to 8192, as said below
- weights: float32 [2, 8192], P('sib', 'col'), may hold values from -5 to 5
- shifts: float32 [2, 256], P('sib'), may hold values from 0 to 8192, as said below
- pair_src: int32 [2, 4, 512], P('sib', 'col'), may hold values from 0 to 2047, as said below
- pair_dst: int32 [2, 4, 512], P('sib', 'col'), may hold values from 0 to 2047, as said below
- rot_cos: float32 [2, 4, 512], P('sib', 'col'), may hold values from 0.3 to 1
- rot_sin: float32 [2, 4, 512], P('sib', 'col'), may hold values from -1 to 1
Outputs:
- merged: bfloat16 [8192, 256], P(('sib', 'row', 'col'))
Inputs may be any that keep to these rules, and one draw needn't show every extreme that they name: Poles are dealt block-cyclically over col: poles[s, c * 2048 + i] equals i * 4 + c plus an offset in [0, 0.25], so every col index holds poles spaced 4 apart over the whole spectrum. shifts[s, j] equals j * 32 + (j % 4) + 0.5 plus an offset in [0, 0.25], so no shift comes within 0.25 of a pole. `pair_src`: for each sibling and col index the 512 entries are distinct local columns; 0 and 2047 are among them. `pair_dst`: for each sibling and col index the 512 entries are distinct local columns; 0 and 2047 are among them.
All inputs are finite; a program needn't handle non-finite values.
Results may differ from a plain program's by a relative error of at most 0.00175.
Values may be sent and summed in bfloat16 or wider, within the bound.
A program may use at most 64 MiB of HBM per device.

v0:
```python
import jax
import jax.numpy as jnp
from jax import lax
from jax.sharding import PartitionSpec as P


def swapped(value, axis, bit):
    mask = 2**bit
    pairs = [(source, source ^ mask) for source in range(lax.axis_size(axis))]
    return lax.ppermute(value, axis, pairs)


def body(eigvec, poles, weights, shifts, pair_src, pair_dst, rot_cos, rot_sin):
    local_vecs = eigvec[0]
    pole_vals = poles[0]
    weight_vals = weights[0]
    shift_vals = shifts[0]
    source = pair_src[0, 0]
    target = pair_dst[0, 0]
    cosines = rot_cos[0, 0]
    sines = rot_sin[0, 0]
    col_width = local_vecs.shape[1]
    col_devices = lax.axis_size("col")
    half_bit = col_devices.bit_length() - 2
    cauchy = weight_vals[:, None] / (pole_vals[:, None] - shift_vals[None, :])
    normsq = lax.psum(jnp.sum(cauchy * cauchy, axis=0), "col")
    cosfull = jnp.ones((col_width,), jnp.float32).at[target].set(cosines)
    cauchy_slab = cauchy * cosfull[:, None]
    rotrows = sines[:, None] * cauchy[target]
    source_cols = local_vecs[:, source]
    left_extra = swapped(source_cols, "col", half_bit)
    own_rows = local_vecs.astype(jnp.float32)
    extra_rows = left_extra.astype(jnp.float32)
    term = jnp.dot(own_rows, cauchy_slab, precision=lax.Precision.HIGHEST)
    summed = lax.psum_scatter(
        term + jnp.dot(extra_rows, rotrows, precision=lax.Precision.HIGHEST),
        "col",
        scatter_dimension=0,
        tiled=True,
    )
    return (summed / jnp.sqrt(normsq)[None, :]).astype(jnp.bfloat16)


def solution(mesh):
    in_specs = (
        P("sib", "row", "col"),
        P("sib", "col"),
        P("sib", "col"),
        P("sib", None),
        P("sib", "col", None),
        P("sib", "col", None),
        P("sib", "col", None),
        P("sib", "col", None),
    )
    out_specs = P(("sib", "row", "col"), None)
    return jax.shard_map(body, mesh=mesh, in_specs=in_specs, out_specs=out_specs, check_vma=False)
```

profile of v0, /device:TPU:0, one launch (start us, length us, event | category | flops | bytes accessed | tf_op | source)
XLA Modules:
  0.0 84.3 jit_solution(18236977403585855117)
XLA Ops:
  6.5 0.0 copy-start.3
  6.5 0.0 reduce-scatter.2.cloned.1.call-start
  6.5 6.4 %copy.12 = bf16[1,1024,2048]{1,2,0:T(8,128)(2,1)} copy(bf16[1,1024,2048]{2,1,0:T(8,128)(2,1)} %param.8) | data formatting | bytes 8388608 | tf_op args[0]
  12.9 0.0 copy-done.3
  13.0 0.0 copy-start.4
  13.0 0.0 copy-start
  13.0 0.0 copy-start.1
  13.0 0.0 copy-start.5
  13.0 6.2 %gather_fusion = bf16[512,1024]{1,0:T(8,128)(2,1)} fusion(bf16[1024,2048]{0,1:T(8,128)(2,1)} %bitcast.21, s32[1024]{0:T(1024)S(1)} %pad_clamp_fusion.1), kind=kCustom, calls=%fused_computation | custom fusion | bytes 2099200 | tf_op jit(solution)/shard_map/gather | solution.py:30
  19.2 2.9 %collective-permute-start = (bf16[1024,512]{0,1:T(8,128)(2,1)}, bf16[1024,512]{0,1:T(8,128)(2,1)}, u32[]{:S(2)}, u32[]{:S(2)}) collective-permute-start(bf16[1024,512]{0,1:T(8,128)(2,1)} %bitcast.10), channel_id=1, source_target_pairs={{0,2},{1,3},{2,0},{3,1},{4,6},{5,7},{6,4},{7,5},{8,10},{9,11},{10,... | collective-permute-start | bytes 3145736 | tf_op jit(solution)/shard_map/ppermute | solution.py:10
  22.2 0.0 copy-done.4
  22.2 2.8 %scatter_custom_fusion = f32[2048]{0:T(1024)S(1)} fusion(s32[512]{0:T(512)S(1)} %bitcast.26, f32[512]{0:T(512)} %bitcast.32, f32[]{:T(128)} %constant.0.clone.1), kind=kCustom, calls=%fused_computation.18 | custom fusion | bytes 8704 | tf_op jit(solution)/shard_map/scatter | solution.py:27
  25.0 0.0 copy-done
  25.0 0.0 copy-done.1
  25.0 0.0 copy-done.5
  25.0 0.6 multiply_reduce_fusion
  25.7 1.6 %gather_fusion.1 = f32[512,256]{1,0:T(8,128)S(1)} fusion(f32[2048,256]{1,0:T(8,128)S(1)} %get-tuple-element.6, s32[1024]{0:T(1024)S(1)} %pad_clamp_fusion), kind=kCustom, calls=%fused_computation.1 | custom fusion | bytes 1050624 | tf_op jit(solution)/shard_map/gather | solution.py:29
  27.2 0.0 copy-start.2
  27.2 9.7 %fusion.3 = f32[1024,256]{0,1:T(8,128)S(1)} fusion(bf16[1,1024,2048]{2,1,0:T(8,128)(2,1)} %param.8, f32[2048]{0:T(1024)S(1)} %scatter_custom_fusion, f32[256]{0:T(256)S(1)} %bitcast.31, f32[2048]{0:T(1024)S(1)} %bitcast.23, f32[2048]{0:T(1024)S(1)} %bitcast.25), kind=kOutput, calls=%fused_computation.8 | convolution fusion | flops 6444023808 | bytes 5268480 | tf_op jit(solution)/shard_map/dot_general | solution.py:34
  37.0 8.7 %collective-permute-done = bf16[1024,512]{0,1:T(8,128)(2,1)} collective-permute-done((bf16[1024,512]{0,1:T(8,128)(2,1)}, bf16[1024,512]{0,1:T(8,128)(2,1)}, u32[]{:S(2)}, u32[]{:S(2)}) %collective-permute-start) | collective-permute-done | bytes 1048608 | tf_op jit(solution)/shard_map/ppermute | solution.py:10
  45.7 0.0 copy-done.2
  45.7 3.4 %convolution_add_fusion = f32[1024,256]{0,1:T(8,128)} fusion(f32[1024,256]{0,1:T(8,128)S(1)} %fusion.3, bf16[1024,512]{0,1:T(8,128)(2,1)} %collective-permute-done, f32[512,256]{1,0:T(8,128)S(1)} %gather_fusion.1, f32[512]{0:T(512)S(1)} %bitcast.29), kind=kOutput, calls=%fused_computation.9 | convolution fusion | flops 1611005952 | bytes 3672064 | tf_op jit(solution)/shard_map/dot_general | solution.py:36
  49.1 0.0 reduce-scatter.2.cloned.1.call-update
  49.1 6.0 %psum.7 = f32[256]{0:T(256)S(1)} all-reduce(f32[256]{0:T(256)S(1)} %get-tuple-element.5), channel_id=1, replica_groups=mesh['sib'=2,'row'=4,'col'=4] {'col'}, use_global_device_ids=true, to_apply=%region_3.0 | all-reduce | flops 256 | bytes 2048 | tf_op jit(solution)/shard_map/psum | solution.py:26
  55.1 20.6 %reduce-scatter.2.cloned.1.call-done = f32[256,256]{0,1:T(8,128)} async-done(((f32[1024,256]{0,1:T(8,128)}), f32[256,256]{0,1:T(8,128)}) %reduce-scatter.2.cloned.1.call-update) | async-done | bytes 262160 | tf_op jit(solution)/shard_map/reduce_scatter | solution.py:35
  75.6 1.1 %divide_convert_fusion = bf16[256,256]{0,1:T(8,128)(2,1)S(1)} fusion(f32[256,256]{0,1:T(8,128)} %reduce-scatter.2.cloned.1.call-done, f32[256]{0:T(256)S(1)} %sqrt.3), kind=kLoop, calls=%fused_computation.12 | loop fusion | flops 131072 | bytes 394240 | tf_op jit(solution)/shard_map/convert_element_type | solution.py:41
  76.7 0.8 copy.14
  (5 shorter events, 0.0 us)
Async XLA Ops:
  6.5 6.4 %copy-start.3 = (s32[1,1,512]{2,1,0:T(1,128)S(1)}, s32[1,1,512]{2,1,0:T(1,128)}, u32[]{:S(2)}) copy-start(s32[1,1,512]{2,1,0:T(1,128)} %param.12) | copy-start | bytes 6148
  6.5 69.1 %reduce-scatter.2.cloned.1.call-start = ((), (), s32[]{:S(2)}) async-start(), calls=%async_computation.1 | async-start | bytes 1310720 | tf_op jit(solution)/shard_map/reduce_scatter | solution.py:35
  13.0 9.2 %copy-start.4 = (s32[1,1,512]{2,1,0:T(1,128)S(1)}, s32[1,1,512]{2,1,0:T(1,128)}, u32[]{:S(2)}) copy-start(s32[1,1,512]{2,1,0:T(1,128)} %param.13) | copy-start | bytes 6148
  13.0 12.0 %copy-start = (f32[1,2048]{1,0:T(1,128)S(1)}, f32[1,2048]{1,0:T(1,128)}, u32[]{:S(2)}) copy-start(f32[1,2048]{1,0:T(1,128)} %param.9) | copy-start | bytes 24580
  13.0 12.0 %copy-start.1 = (f32[1,2048]{1,0:T(1,128)S(1)}, f32[1,2048]{1,0:T(1,128)}, u32[]{:S(2)}) copy-start(f32[1,2048]{1,0:T(1,128)} %param.10) | copy-start | bytes 24580
  13.0 12.0 %copy-start.5 = (f32[1,256]{1,0:T(1,128)S(1)}, f32[1,256]{1,0:T(1,128)}, u32[]{:S(2)}) copy-start(f32[1,256]{1,0:T(1,128)} %param.11) | copy-start | bytes 3076
  19.2 26.4 %collective-permute-start = (bf16[1024,512]{0,1:T(8,128)(2,1)}, bf16[1024,512]{0,1:T(8,128)(2,1)}, u32[]{:S(2)}, u32[]{:S(2)}) collective-permute-start(bf16[1024,512]{0,1:T(8,128)(2,1)} %bitcast.10), channel_id=1, source_target_pairs={{0,2},{1,3},{2,0},{3,1},{4,6},{5,7},{6,4},{7,5},{8,10},{9,11},{10,... | collective-permute-start | bytes 3145736 | tf_op jit(solution)/shard_map/ppermute | solution.py:10
  27.2 18.4 %copy-start.2 = (f32[1,1,512]{2,1,0:T(1,128)S(1)}, f32[1,1,512]{2,1,0:T(1,128)}, u32[]{:S(2)}) copy-start(f32[1,1,512]{2,1,0:T(1,128)} %param.15) | copy-start | bytes 6148
Sparse Core Ops, SparseCore 0:
  49.2 26.3 reduce-scatter.1
where the time goes:
time: 84.7 us; the launch traced here: 84.3 us
  waiting for transfers between devices  29.2 us (34%)
  local copies, waits for them, and re-layouts  17.8 us (21%)
  between operations  13.5 us (16%)
  matrix products  13.1 us (15%)
  blocking collectives  5.96 us (7%)
  starting transfers between devices  2.94 us (3%)
  other arithmetic  1.69 us (2%)
    reduce_scatter x1, waiting for transfers between devices, body(): lax.psum_scatter(term + jnp.dot(extra_rows, rotrows, precision=lax.Precis...  20.6 us
    dot_general x1, matrix products, body(): term = jnp.dot(own_rows, cauchy_slab, precision=lax.Precision.HIGHEST)  9.73 us
    ppermute x1, waiting for transfers between devices, swapped(): return lax.ppermute(value, axis, pairs)  8.67 us
    unnamed x13, local copies, waits for them, and re-layouts  6.44 us
    gather x1, local copies, waits for them, and re-layouts, body(): source_cols = local_vecs[:, source]  6.23 us
    psum x1, blocking collectives, body(): normsq = lax.psum(jnp.sum(cauchy * cauchy, axis=0), 'col')  5.96 us
    dot_general x1, matrix products, body(): jnp.dot(extra_rows, rotrows, precision=lax.Precision.HIGHEST)  3.39 us
    ppermute x1, starting transfers between devices, swapped(): return lax.ppermute(value, axis, pairs)  2.94 us
  transfers between devices with their start and end apart: 2, of which 2 were waited for; matrix products, arithmetic and copies ran while one was open for 17% of the time, Pallas kernels for 0%

commit v1 on v0

v1 whole, which is shorter than its diff:
```python
import functools

import jax
import jax.numpy as jnp
from jax import lax
from jax.experimental import pallas as pl
from jax.experimental.pallas import tpu as pltpu
from jax.sharding import PartitionSpec as P

LANES = 128
SUB = 64
MESH = pl.DeviceIdType.MESH


def inverse(value):
    guess = pl.reciprocal(value, approx=True)
    return guess * (2.0 - value * guess)


def pick(tables, index):
    row, lane = index >> 7, index & (LANES - 1)
    picked = jnp.zeros(index.shape, jnp.float32)
    for t, table in enumerate(tables):
        there = jnp.take_along_axis(jnp.broadcast_to(table, index.shape), lane, axis=1)
        picked = jnp.where(row == t, there, picked)
    return picked


def kernel(n, eig, poles, weights, shifts, src, dst, cosines, sines, out,
           eig_buf, slab_own, slab_hi, slab_lo, shift_t, src_t, dst_t, cos_t, listed, inv,
           part_b, part_q, norm_acc, pair_send, pair_recv, norm_send, norm_recv,
           core_send, core_recv, chip_send, chip_recv,
           eig_sem, pair_ssem, pair_rsem, norm_ssem, norm_rsem,
           core_ssem, core_rsem, chip_ssem, chip_rsem):
    rows, width = eig_buf.shape
    block = rows // n
    slab = shifts.shape[1]
    pairs = src.shape[2]
    tiles, lists = width // LANES, pairs // LANES
    chips = n // 2
    me = lax.axis_index("col")
    chip, core = me // 2, lax.rem(me, 2)
    other = 1 - core

    def col(index):
        return {"col": index}

    def peer(step):
        return lax.rem(me + step, n)

    barrier = pltpu.get_barrier_semaphore()
    for step in range(1, n):
        pl.semaphore_signal(barrier, inc=1, device_id=col(peer(step)), device_id_type=MESH)

    loads = []
    for part in range(4):
        span = pl.ds(part * (rows // 4), rows // 4)
        load = pltpu.make_async_copy(eig.at[0, span, :], eig_buf.at[span, :], eig_sem.at[part])
        load.start()
        loads.append(load)

    listed[...] = jnp.zeros_like(listed)
    for r in range(lists):
        cut = slice(r * LANES, (r + 1) * LANES)
        listed[r:r + 1, :] = dst[0, :, cut]
    index = listed[...]
    pole_rows = [poles[:, t * LANES:(t + 1) * LANES] for t in range(tiles)]
    weight_rows = [weights[:, t * LANES:(t + 1) * LANES] for t in range(tiles)]
    pair_send[0] = pick(weight_rows, index)
    pair_send[1] = pick(pole_rows, index)
    for r in range(lists):
        cut = slice(r * LANES, (r + 1) * LANES)
        pair_send[0, r:r + 1, :] = pair_send[0, r:r + 1, :] * sines[0, :, cut]

    pl.semaphore_wait(barrier, n - 1)
    pair_copy = pltpu.make_async_remote_copy(
        src_ref=pair_send, dst_ref=pair_recv, send_sem=pair_ssem, recv_sem=pair_rsem,
        device_id=col(lax.rem(me + n // 2, n)), device_id_type=MESH)
    pair_copy.start()

    for r in range(lists):
        cut = slice(r * LANES, (r + 1) * LANES)
        src_t[cut, :] = jnp.broadcast_to(src[0, :, cut], (LANES, LANES)).T
        dst_t[cut, :] = jnp.broadcast_to(dst[0, :, cut], (LANES, LANES)).T
        cos_t[cut, :] = jnp.broadcast_to(cosines[0, :, cut], (LANES, LANES)).T - 1.0
    for r in range(slab // LANES):
        cut = slice(r * LANES, (r + 1) * LANES)
        shift_t[cut, :] = jnp.broadcast_to(shifts[:, cut], (LANES, LANES)).T
    norm_acc[...] = jnp.zeros_like(norm_acc)

    def own_part(t, carry):
        cut = pl.ds(pl.multiple_of(t * LANES, LANES), LANES)
        local = lax.broadcasted_iota(jnp.int32, (SUB, LANES), 1) + t * LANES
        turned = jnp.zeros((SUB, LANES), jnp.float32)
        place = jnp.zeros((SUB, LANES), jnp.int32)
        count = lax.broadcasted_iota(jnp.int32, (SUB, LANES), 0) + 1
        for r in range(0, pairs, SUB):
            turned = jnp.where(dst_t[r:r + SUB, :] == local, cos_t[r:r + SUB, :], turned)
            place = jnp.where(src_t[r:r + SUB, :] == local, count + r, place)
        cosfull = 1.0 + jnp.sum(turned, axis=0, keepdims=True)
        inv[pl.ds(t, 1), :] = jnp.sum(place, axis=0, keepdims=True)
        pole = poles[:, cut]
        weight = weights[:, cut]
        for r in range(0, slab, SUB):
            cauchy = weight * inverse(pole - shift_t[r:r + SUB, :])
            norm_acc[r:r + SUB, :] += cauchy * cauchy
            slab_own[r:r + SUB, cut] = cosfull * cauchy
        return carry

    lax.fori_loop(0, tiles, own_part, 0)

    norm_send[...] = jnp.broadcast_to(jnp.sum(norm_acc[...].T, axis=0, keepdims=True), norm_send.shape)
    norm_copies = []
    for step in range(1, n):
        copy = pltpu.make_async_remote_copy(
            src_ref=norm_send, dst_ref=norm_recv.at[step], send_sem=norm_ssem.at[step],
            recv_sem=norm_rsem.at[step], device_id=col(peer(step)), device_id_type=MESH)
        copy.start()
        norm_copies.append(copy)

    pair_copy.wait()
    for t in range(0, tiles, 8):
        place = inv[t:t + 8, :]
        at = jnp.maximum(place - 1, 0)
        part_b[t:t + 8, :] = jnp.where(place > 0, pick([pair_recv[0, r:r + 1, :] for r in range(lists)], at), 0.0)
        part_q[t:t + 8, :] = jnp.where(place > 0, pick([pair_recv[1, r:r + 1, :] for r in range(lists)], at), -1.0)

    def partner_part(t, carry):
        cut = pl.ds(pl.multiple_of(t * LANES, LANES), LANES)
        pole = part_q[pl.ds(t, 1), :]
        weight = part_b[pl.ds(t, 1), :]
        for r in range(0, slab, SUB):
            total = slab_own[r:r + SUB, cut] + weight * inverse(pole - shift_t[r:r + SUB, :])
            high = total.astype(jnp.bfloat16)
            slab_hi[r:r + SUB, cut] = high
            slab_lo[r:r + SUB, cut] = (total - high.astype(jnp.float32)).astype(jnp.bfloat16)
        return carry

    lax.fori_loop(0, tiles, partner_part, 0)

    for load in loads:
        load.wait()

    def product(owner):
        left = eig_buf[pl.ds(pl.multiple_of(owner * block, block), block), :]
        dims = (((1,), (1,)), ((), ()))
        return (lax.dot_general(left, slab_hi[...], dims, preferred_element_type=jnp.float32)
                + lax.dot_general(left, slab_lo[...], dims, preferred_element_type=jnp.float32))

    core_copies, chip_copies = [], []

    def to_core(step, owner_chip):
        core_send[step] = product(owner_chip * 2 + other)
        copy = pltpu.make_async_remote_copy(
            src_ref=core_send.at[step], dst_ref=core_recv.at[step], send_sem=core_ssem.at[step],
            recv_sem=core_rsem.at[step], device_id=col(chip * 2 + other), device_id_type=MESH)
        copy.start()
        core_copies.append(copy)

    for step in range(1, chips):
        away = lax.rem(chip + step, chips)
        to_core(step, away)
        mine = product(away * 2 + core)
        core_copies[-1].wait_recv()
        chip_send[step] = mine + core_recv[step]
        copy = pltpu.make_async_remote_copy(
            src_ref=chip_send.at[step], dst_ref=chip_recv.at[step], send_sem=chip_ssem.at[step],
            recv_sem=chip_rsem.at[step], device_id=col(away * 2 + core), device_id_type=MESH)
        copy.start()
        chip_copies.append(copy)
    to_core(0, chip)
    total = product(me)
    core_copies[-1].wait_recv()
    chip_send[0] = total + core_recv[0]

    normsq = norm_send[0:1, :]
    for step, copy in enumerate(norm_copies):
        copy.wait()
        normsq = normsq + norm_recv[step + 1, 0:1, :]
    scale = jnp.sqrt(normsq)
    for copy in chip_copies:
        copy.wait()
    total = chip_send[0]
    for step in range(1, chips):
        total = total + chip_recv[step]
    out[...] = (total / scale).astype(out.dtype)
    for copy in core_copies:
        copy.wait_send()


def body(eigvec, *small):
    n = lax.axis_size("col")
    _, rows, width = eigvec.shape
    slab = small[2].shape[1]
    pairs = small[3].shape[2]
    block = rows // n
    chips = n // 2
    tiles = width // LANES
    f32, bf16 = jnp.float32, jnp.bfloat16
    vmem = pl.BlockSpec(memory_space=pltpu.VMEM)
    dma = pltpu.SemaphoreType.DMA
    return pl.pallas_call(
        functools.partial(kernel, n),
        out_shape=jax.ShapeDtypeStruct((block, slab), bf16),
        in_specs=[pl.BlockSpec(memory_space=pl.ANY)] + [vmem] * 7,
        out_specs=vmem,
        scratch_shapes=[
            pltpu.VMEM((rows, width), bf16),
            pltpu.VMEM((slab, width), f32),
            pltpu.VMEM((slab, width), bf16),
            pltpu.VMEM((slab, width), bf16),
            pltpu.VMEM((slab, LANES), f32),
            pltpu.VMEM((pairs, LANES), jnp.int32),
            pltpu.VMEM((pairs, LANES), jnp.int32),
            pltpu.VMEM((pairs, LANES), f32),
            pltpu.VMEM((8, LANES), jnp.int32),
            pltpu.VMEM((tiles, LANES), jnp.int32),
            pltpu.VMEM((tiles, LANES), f32),
            pltpu.VMEM((tiles, LANES), f32),
            pltpu.VMEM((slab, LANES), f32),
            pltpu.VMEM((2, 8, LANES), f32),
            pltpu.VMEM((2, 8, LANES), f32),
            pltpu.VMEM((8, slab), f32),
            pltpu.VMEM((n, 8, slab), f32),
            pltpu.VMEM((chips, block, slab), f32),
            pltpu.VMEM((chips, block, slab), f32),
            pltpu.VMEM((chips, block, slab), f32),
            pltpu.VMEM((chips, block, slab), f32),
            dma((4,)), dma, dma, dma((n,)), dma((n,)),
            dma((chips,)), dma((chips,)), dma((chips,)), dma((chips,)),
        ],
        compiler_params=pltpu.CompilerParams(
            collective_id=0, has_side_effects=True, vmem_limit_bytes=40 * 2**20),
        cost_estimate=pl.CostEstimate(
            flops=4 * rows * width * slab, bytes_accessed=2 * rows * width, transcendentals=2 * width * slab),
        name="merge",
    )(eigvec, *small)


def solution(mesh):
    in_specs = (
        P("sib", "row", "col"),
        P("sib", "col"),
        P("sib", "col"),
        P("sib", None),
        P("sib", "col", None),
        P("sib", "col", None),
        P("sib", "col", None),
        P("sib", "col", None),
    )
    out_specs = P(("sib", "row", "col"), None)
    return jax.shard_map(body, mesh=mesh, in_specs=in_specs, out_specs=out_specs, check_vma=False)
```

time: 84.7 us -> 25.2 us (0.30)
  waiting for transfers between devices: 29.2 us -> 0 us
  Pallas kernels: 0 us -> 17.2 us
  between operations: 13.5 us -> 0.02 us
  matrix products: 13.1 us -> 0 us
  local copies, waits for them, and re-layouts: 17.8 us -> 7.64 us
  blocking collectives: 5.96 us -> 0 us
  starting transfers between devices: 2.94 us -> 0 us
  other arithmetic: 1.69 us -> 0 us
    reduce_scatter x1 -> x0, waiting for transfers between devices: 20.6 us -> none  [body(): lax.psum_scatter(term + jnp.dot(extra_rows, rotrows, precision=lax.Precis...]
    pallas_call x0 -> x1, Pallas kernels: none -> 17.2 us  [body(): pl.pallas_call(functools.partial(kernel, n), out_shape=jax.ShapeDtypeStru...]
    dot_general x2 -> x0, matrix products: 13.1 us -> none  [the longest x1 9.73 us: body(): term = jnp.dot(own_rows, cauchy_slab, precision=lax.Precision.HIGHEST)]
    ppermute x1 -> x0, waiting for transfers between devices: 8.67 us -> none  [swapped(): return lax.ppermute(value, axis, pairs)]
    gather x2 -> x0, local copies, waits for them, and re-layouts: 7.8 us -> none  [the longest x1 6.23 us: body(): source_cols = local_vecs[:, source]]
    psum x1 -> x0, blocking collectives: 5.96 us -> none  [body(): normsq = lax.psum(jnp.sum(cauchy * cauchy, axis=0), 'col')]
    ppermute x1 -> x0, starting transfers between devices: 2.94 us -> none  [swapped(): return lax.ppermute(value, axis, pairs)]
    scatter x1 -> x0, local copies, waits for them, and re-layouts: 2.79 us -> none  [body(): cosfull = jnp.ones((col_width,), jnp.float32).at[target].set(cosines)]
  transfers between devices with their start and end apart: 2 -> 0, of which waited for: 2 -> 0; matrix products, arithmetic and copies ran while one was open for 17% -> 0% of each run, Pallas kernels for 0% -> 0%
where the time goes in v1:
time: 25.2 us; the launch traced here: 24.9 us
  Pallas kernels  17.2 us (68%)
  local copies, waits for them, and re-layouts  7.64 us (30%)
    pallas_call x1, Pallas kernels, body(): pl.pallas_call(functools.partial(kernel, n), out_shape=jax.ShapeDtypeStru...  17.2 us
    unnamed x17, local copies, waits for them, and re-layouts  7.64 us

profile of v1, /device:TPU:0, one launch (start us, length us, event | category | flops | bytes accessed | tf_op | source)
XLA Modules:
  0.0 24.9 jit_solution(2242833374730658175)
XLA Ops:
  0.0 0.0 copy-start
  0.0 2.2 %copy-done = bf16[1,1024,2048]{2,1,0:T(8,128)(2,1)S(1)} copy-done((bf16[1,1024,2048]{2,1,0:T(8,128)(2,1)S(1)}, bf16[1,1024,2048]{2,1,0:T(8,128)(2,1)}, u32[]{:S(2)}) %copy-start) | copy-done | bytes 4194328
  2.2 0.0 copy-start.1
  2.2 0.7 %copy-done.1 = f32[1,2048]{1,0:T(1,128)S(1)} copy-done((f32[1,2048]{1,0:T(1,128)S(1)}, f32[1,2048]{1,0:T(1,128)}, u32[]{:S(2)}) %copy-start.1) | copy-done | bytes 8216
  2.9 0.0 copy-start.2
  2.9 0.7 %copy-done.2 = f32[1,2048]{1,0:T(1,128)S(1)} copy-done((f32[1,2048]{1,0:T(1,128)S(1)}, f32[1,2048]{1,0:T(1,128)}, u32[]{:S(2)}) %copy-start.2) | copy-done | bytes 8216
  3.6 0.0 copy-start.3
  3.6 0.7 %copy-done.3 = s32[1,1,512]{2,1,0:T(1,128)S(1)} copy-done((s32[1,1,512]{2,1,0:T(1,128)S(1)}, s32[1,1,512]{2,1,0:T(1,128)}, u32[]{:S(2)}) %copy-start.3) | copy-done | bytes 2072
  4.3 0.0 copy-start.4
  4.3 0.7 %copy-done.4 = s32[1,1,512]{2,1,0:T(1,128)S(1)} copy-done((s32[1,1,512]{2,1,0:T(1,128)S(1)}, s32[1,1,512]{2,1,0:T(1,128)}, u32[]{:S(2)}) %copy-start.4) | copy-done | bytes 2072
  4.9 0.0 copy-start.5
  5.0 0.7 %copy-done.5 = f32[1,1,512]{2,1,0:T(1,128)S(1)} copy-done((f32[1,1,512]{2,1,0:T(1,128)S(1)}, f32[1,1,512]{2,1,0:T(1,128)}, u32[]{:S(2)}) %copy-start.5) | copy-done | bytes 2072
  5.6 0.0 copy-start.6
  5.6 0.7 %copy-done.6 = f32[1,1,512]{2,1,0:T(1,128)S(1)} copy-done((f32[1,1,512]{2,1,0:T(1,128)S(1)}, f32[1,1,512]{2,1,0:T(1,128)}, u32[]{:S(2)}) %copy-start.6) | copy-done | bytes 2072
  6.3 0.0 copy-start.7
  6.3 0.7 %copy-done.7 = f32[1,256]{1,0:T(1,128)S(1)} copy-done((f32[1,256]{1,0:T(1,128)S(1)}, f32[1,256]{1,0:T(1,128)}, u32[]{:S(2)}) %copy-start.7) | copy-done | bytes 1048
  7.0 17.2 %merge.1 = bf16[256,256]{1,0:T(8,128)(2,1)S(1)} custom-call(bf16[1,1024,2048]{2,1,0:T(8,128)(2,1)S(1)} %copy-done, f32[1,2048]{1,0:T(1,128)S(1)} %copy-done.1, f32[1,2048]{1,0:T(1,128)S(1)} %copy-done.2, f32[1,256]{1,0:T(1,128)S(1)} %copy-done.7, s32[1,1,512]{2,1,0:T(1,128)S(1)} %copy-done.3, s32[1,1,512]{2,1,0:T(1,128)S(1)} %copy-done.4, ...), custom_call_target="tpu_custom_call" | custom-call | flops 2147483648 | bytes 4194304 | tf_op jit(solution)/shard_map/merge/pallas_call | solution.py:202
  24.2 0.7 %copy.10 = bf16[256,256]{1,0:T(8,128)(2,1)} copy(bf16[256,256]{1,0:T(8,128)(2,1)S(1)} %merge.1) | data formatting | bytes 262144
Async XLA Ops:
  0.0 2.2 %copy-start = (bf16[1,1024,2048]{2,1,0:T(8,128)(2,1)S(1)}, bf16[1,1024,2048]{2,1,0:T(8,128)(2,1)}, u32[]{:S(2)}) copy-start(bf16[1,1024,2048]{2,1,0:T(8,128)(2,1)} %eig.1) | copy-start | bytes 12582916
  2.2 0.7 %copy-start.1 = (f32[1,2048]{1,0:T(1,128)S(1)}, f32[1,2048]{1,0:T(1,128)}, u32[]{:S(2)}) copy-start(f32[1,2048]{1,0:T(1,128)} %poles.1) | copy-start | bytes 24580
  2.9 0.7 %copy-start.2 = (f32[1,2048]{1,0:T(1,128)S(1)}, f32[1,2048]{1,0:T(1,128)}, u32[]{:S(2)}) copy-start(f32[1,2048]{1,0:T(1,128)} %weights.1) | copy-start | bytes 24580
  3.6 0.7 %copy-start.3 = (s32[1,1,512]{2,1,0:T(1,128)S(1)}, s32[1,1,512]{2,1,0:T(1,128)}, u32[]{:S(2)}) copy-start(s32[1,1,512]{2,1,0:T(1,128)} %src.1) | copy-start | bytes 6148
  4.3 0.7 %copy-start.4 = (s32[1,1,512]{2,1,0:T(1,128)S(1)}, s32[1,1,512]{2,1,0:T(1,128)}, u32[]{:S(2)}) copy-start(s32[1,1,512]{2,1,0:T(1,128)} %dst.1) | copy-start | bytes 6148
  4.9 0.7 %copy-start.5 = (f32[1,1,512]{2,1,0:T(1,128)S(1)}, f32[1,1,512]{2,1,0:T(1,128)}, u32[]{:S(2)}) copy-start(f32[1,1,512]{2,1,0:T(1,128)} %cosines.1) | copy-start | bytes 6148
  5.6 0.7 %copy-start.6 = (f32[1,1,512]{2,1,0:T(1,128)S(1)}, f32[1,1,512]{2,1,0:T(1,128)}, u32[]{:S(2)}) copy-start(f32[1,1,512]{2,1,0:T(1,128)} %sines.1) | copy-start | bytes 6148
  6.3 0.7 %copy-start.7 = (f32[1,256]{1,0:T(1,128)S(1)}, f32[1,256]{1,0:T(1,128)}, u32[]{:S(2)}) copy-start(f32[1,256]{1,0:T(1,128)} %shifts.1) | copy-start | bytes 3076

commit v2 on v1

--- a/solution.py
+++ b/solution.py
@@ -26,12 +26,14 @@
     return picked
 
 
-def kernel(n, eig, poles, weights, shifts, src, dst, cosines, sines, out,
-           eig_buf, slab_own, slab_hi, slab_lo, shift_t, src_t, dst_t, cos_t, listed, inv,
-           part_b, part_q, norm_acc, pair_send, pair_recv, norm_send, norm_recv,
-           core_send, core_recv, chip_send, chip_recv,
-           eig_sem, pair_ssem, pair_rsem, norm_ssem, norm_rsem,
-           core_ssem, core_rsem, chip_ssem, chip_rsem):
+def kernel(n, eig, *refs):
+    small_hbm, out, small = refs[:7], refs[7], refs[8:15]
+    poles, weights, shifts, src, dst, cosines, sines = small
+    (eig_buf, slab_own, slab_hi, slab_lo, shift_t, src_t, dst_t, cos_t, listed, inv,
+     part_b, part_q, norm_acc, pair_send, pair_recv, norm_send, norm_recv,
+     core_send, core_recv, chip_send, chip_recv,
+     eig_sem, pair_ssem, pair_rsem, norm_ssem, norm_rsem,
+     core_ssem, core_rsem, chip_ssem, chip_rsem, small_sem) = refs[15:]
     rows, width = eig_buf.shape
     block = rows // n
     slab = shifts.shape[1]
@@ -48,6 +50,12 @@
     def peer(step):
         return lax.rem(me + step, n)
 
+    small_loads = []
+    for at, (source, target) in enumerate(zip(small_hbm, small)):
+        load = pltpu.make_async_copy(source, target, small_sem.at[at])
+        load.start()
+        small_loads.append(load)
+
     barrier = pltpu.get_barrier_semaphore()
     for step in range(1, n):
         pl.semaphore_signal(barrier, inc=1, device_id=col(peer(step)), device_id_type=MESH)
@@ -58,6 +66,9 @@
         load = pltpu.make_async_copy(eig.at[0, span, :], eig_buf.at[span, :], eig_sem.at[part])
         load.start()
         loads.append(load)
+
+    for load in small_loads:
+        load.wait()
 
     listed[...] = jnp.zeros_like(listed)
     for r in range(lists):
@@ -202,9 +213,10 @@
     return pl.pallas_call(
         functools.partial(kernel, n),
         out_shape=jax.ShapeDtypeStruct((block, slab), bf16),
-        in_specs=[pl.BlockSpec(memory_space=pl.ANY)] + [vmem] * 7,
+        in_specs=[pl.BlockSpec(memory_space=pltpu.HBM)] * 8,
         out_specs=vmem,
         scratch_shapes=[
+            *(pltpu.VMEM(value.shape, value.dtype) for value in small),
             pltpu.VMEM((rows, width), bf16),
             pltpu.VMEM((slab, width), f32),
             pltpu.VMEM((slab, width), bf16),
@@ -227,7 +239,7 @@
             pltpu.VMEM((chips, block, slab), f32),
             pltpu.VMEM((chips, block, slab), f32),
             dma((4,)), dma, dma, dma((n,)), dma((n,)),
-            dma((chips,)), dma((chips,)), dma((chips,)), dma((chips,)),
+            dma((chips,)), dma((chips,)), dma((chips,)), dma((chips,)), dma((7,)),
         ],
         compiler_params=pltpu.CompilerParams(
             collective_id=0, has_side_effects=True, vmem_limit_bytes=40 * 2**20),

time: 25.2 us -> 25.3 us (level)
  no operation moved by 1% of the time
where the time goes in v2:
time: 25.3 us; the launch traced here: 25 us
  Pallas kernels  17.3 us (68%)
  local copies, waits for them, and re-layouts  7.64 us (30%)
    pallas_call x1, Pallas kernels, body(): pl.pallas_call(functools.partial(kernel, n), out_shape=jax.ShapeDtypeStru...  17.3 us
    unnamed x17, local copies, waits for them, and re-layouts  7.64 us

profile of v2, /device:TPU:0, one launch (start us, length us, event | category | flops | bytes accessed | tf_op | source)
XLA Modules:
  0.0 25.0 jit_solution(16492064969504489883)
XLA Ops:
  0.0 0.0 copy-start
  0.0 2.2 %copy-done = bf16[1,1024,2048]{2,1,0:T(8,128)(2,1)S(1)} copy-done((bf16[1,1024,2048]{2,1,0:T(8,128)(2,1)S(1)}, bf16[1,1024,2048]{2,1,0:T(8,128)(2,1)}, u32[]{:S(2)}) %copy-start) | copy-done | bytes 4194328
  2.2 0.0 copy-start.1
  2.2 0.7 %copy-done.1 = f32[1,2048]{1,0:T(1,128)S(1)} copy-done((f32[1,2048]{1,0:T(1,128)S(1)}, f32[1,2048]{1,0:T(1,128)}, u32[]{:S(2)}) %copy-start.1) | copy-done | bytes 8216
  2.9 0.0 copy-start.2
  2.9 0.7 %copy-done.2 = f32[1,2048]{1,0:T(1,128)S(1)} copy-done((f32[1,2048]{1,0:T(1,128)S(1)}, f32[1,2048]{1,0:T(1,128)}, u32[]{:S(2)}) %copy-start.2) | copy-done | bytes 8216
  3.6 0.0 copy-start.3
  3.6 0.7 %copy-done.3 = s32[1,1,512]{2,1,0:T(1,128)S(1)} copy-done((s32[1,1,512]{2,1,0:T(1,128)S(1)}, s32[1,1,512]{2,1,0:T(1,128)}, u32[]{:S(2)}) %copy-start.3) | copy-done | bytes 2072
  4.3 0.0 copy-start.4
  4.3 0.7 %copy-done.4 = s32[1,1,512]{2,1,0:T(1,128)S(1)} copy-done((s32[1,1,512]{2,1,0:T(1,128)S(1)}, s32[1,1,512]{2,1,0:T(1,128)}, u32[]{:S(2)}) %copy-start.4) | copy-done | bytes 2072
  4.9 0.0 copy-start.5
  5.0 0.7 %copy-done.5 = f32[1,1,512]{2,1,0:T(1,128)S(1)} copy-done((f32[1,1,512]{2,1,0:T(1,128)S(1)}, f32[1,1,512]{2,1,0:T(1,128)}, u32[]{:S(2)}) %copy-start.5) | copy-done | bytes 2072
  5.6 0.0 copy-start.6
  5.6 0.7 %copy-done.6 = f32[1,1,512]{2,1,0:T(1,128)S(1)} copy-done((f32[1,1,512]{2,1,0:T(1,128)S(1)}, f32[1,1,512]{2,1,0:T(1,128)}, u32[]{:S(2)}) %copy-start.6) | copy-done | bytes 2072
  6.3 0.0 copy-start.7
  6.3 0.7 %copy-done.7 = f32[1,256]{1,0:T(1,128)S(1)} copy-done((f32[1,256]{1,0:T(1,128)S(1)}, f32[1,256]{1,0:T(1,128)}, u32[]{:S(2)}) %copy-start.7) | copy-done | bytes 1048
  7.0 17.3 %merge.1 = bf16[256,256]{1,0:T(8,128)(2,1)S(1)} custom-call(bf16[1,1024,2048]{2,1,0:T(8,128)(2,1)S(1)} %copy-done, f32[1,2048]{1,0:T(1,128)S(1)} %copy-done.1, f32[1,2048]{1,0:T(1,128)S(1)} %copy-done.2, f32[1,256]{1,0:T(1,128)S(1)} %copy-done.7, s32[1,1,512]{2,1,0:T(1,128)S(1)} %copy-done.3, s32[1,1,512]{2,1,0:T(1,128)S(1)} %copy-done.4, ...), custom_call_target="tpu_custom_call" | custom-call | flops 2147483648 | bytes 4194304 | tf_op jit(solution)/shard_map/merge/pallas_call | solution.py:213
  24.3 0.7 %copy.10 = bf16[256,256]{1,0:T(8,128)(2,1)} copy(bf16[256,256]{1,0:T(8,128)(2,1)S(1)} %merge.1) | data formatting | bytes 262144
Async XLA Ops:
  0.0 2.2 %copy-start = (bf16[1,1024,2048]{2,1,0:T(8,128)(2,1)S(1)}, bf16[1,1024,2048]{2,1,0:T(8,128)(2,1)}, u32[]{:S(2)}) copy-start(bf16[1,1024,2048]{2,1,0:T(8,128)(2,1)} %eig.1) | copy-start | bytes 12582916
  2.2 0.7 %copy-start.1 = (f32[1,2048]{1,0:T(1,128)S(1)}, f32[1,2048]{1,0:T(1,128)}, u32[]{:S(2)}) copy-start(f32[1,2048]{1,0:T(1,128)} %refs_0_.1) | copy-start | bytes 24580
  2.9 0.7 %copy-start.2 = (f32[1,2048]{1,0:T(1,128)S(1)}, f32[1,2048]{1,0:T(1,128)}, u32[]{:S(2)}) copy-start(f32[1,2048]{1,0:T(1,128)} %refs_1_.1) | copy-start | bytes 24580
  3.6 0.7 %copy-start.3 = (s32[1,1,512]{2,1,0:T(1,128)S(1)}, s32[1,1,512]{2,1,0:T(1,128)}, u32[]{:S(2)}) copy-start(s32[1,1,512]{2,1,0:T(1,128)} %refs_3_.1) | copy-start | bytes 6148
  4.3 0.7 %copy-start.4 = (s32[1,1,512]{2,1,0:T(1,128)S(1)}, s32[1,1,512]{2,1,0:T(1,128)}, u32[]{:S(2)}) copy-start(s32[1,1,512]{2,1,0:T(1,128)} %refs_4_.1) | copy-start | bytes 6148
  4.9 0.7 %copy-start.5 = (f32[1,1,512]{2,1,0:T(1,128)S(1)}, f32[1,1,512]{2,1,0:T(1,128)}, u32[]{:S(2)}) copy-start(f32[1,1,512]{2,1,0:T(1,128)} %refs_5_.1) | copy-start | bytes 6148
  5.6 0.7 %copy-start.6 = (f32[1,1,512]{2,1,0:T(1,128)S(1)}, f32[1,1,512]{2,1,0:T(1,128)}, u32[]{:S(2)}) copy-start(f32[1,1,512]{2,1,0:T(1,128)} %refs_6_.1) | copy-start | bytes 6148
  6.3 0.7 %copy-start.7 = (f32[1,256]{1,0:T(1,128)S(1)}, f32[1,256]{1,0:T(1,128)}, u32[]{:S(2)}) copy-start(f32[1,256]{1,0:T(1,128)} %refs_2_.1) | copy-start | bytes 3076

commit v3 on v2

--- a/solution.py
+++ b/solution.py
@@ -242,7 +242,7 @@
             dma((chips,)), dma((chips,)), dma((chips,)), dma((chips,)), dma((7,)),
         ],
         compiler_params=pltpu.CompilerParams(
-            collective_id=0, has_side_effects=True, vmem_limit_bytes=40 * 2**20),
+            collective_id=0, has_side_effects=True, vmem_limit_bytes=60 * 2**20),
         cost_estimate=pl.CostEstimate(
             flops=4 * rows * width * slab, bytes_accessed=2 * rows * width, transcendentals=2 * width * slab),
         name="merge",

time: 25.3 us -> 19.7 us (0.78)
  local copies, waits for them, and re-layouts: 7.64 us -> 1.57 us
  Pallas kernels: 17.3 us -> 17.9 us
    unnamed x17 -> x1, local copies, waits for them, and re-layouts: 7.64 us -> 1.57 us
    pallas_call x1, Pallas kernels: 17.3 us -> 17.9 us  [body(): pl.pallas_call(functools.partial(kernel, n), out_shape=jax.ShapeDtypeStru...]
where the time goes in v3:
time: 19.7 us; the launch traced here: 19.5 us
  Pallas kernels  17.9 us (91%)
  local copies, waits for them, and re-layouts  1.57 us (8%)
    pallas_call x1, Pallas kernels, body(): pl.pallas_call(functools.partial(kernel, n), out_shape=jax.ShapeDtypeStru...  17.9 us
    unnamed x1, local copies, waits for them, and re-layouts  1.57 us

profile of v3, /device:TPU:0, one launch (start us, length us, event | category | flops | bytes accessed | tf_op | source)
XLA Modules:
  0.0 19.5 jit_solution(10643345008555388854)
XLA Ops:
  0.0 17.9 %merge.1 = bf16[256,256]{1,0:T(8,128)(2,1)} custom-call(bf16[1,1024,2048]{2,1,0:T(8,128)(2,1)} %eig.1, f32[1,2048]{1,0:T(1,128)} %refs_0_.1, f32[1,2048]{1,0:T(1,128)} %refs_1_.1, f32[1,256]{1,0:T(1,128)} %refs_2_.1, s32[1,1,512]{2,1,0:T(1,128)} %refs_3_.1, s32[1,1,512]{2,1,0:T(1,128)} %refs_4_.1, f32[1,1,512]{2,1,0:T(1,128)} %refs_5_.1, f32[1,1,512]{2,1,0:T(1,128)} %refs_6_.1), custom_call_target="tpu_custom_call" | custom-call | flops 2147483648 | bytes 4194304 | tf_op jit(solution)/shard_map/merge/pallas_call | solution.py:213
  17.9 1.6 %copy.10 = bf16[256,256]{1,0:T(8,128)(2,1)} copy(bf16[256,256]{1,0:T(8,128)(2,1)} %merge.1) | data formatting | bytes 262144

commit v4 on v3

--- a/solution.py
+++ b/solution.py
@@ -9,6 +9,8 @@
 
 LANES = 128
 SUB = 64
+PARTS = 2
+STEPS = 32767.0
 MESH = pl.DeviceIdType.MESH
 
 
@@ -31,11 +33,12 @@
     poles, weights, shifts, src, dst, cosines, sines = small
     (eig_buf, slab_own, slab_hi, slab_lo, shift_t, src_t, dst_t, cos_t, listed, inv,
      part_b, part_q, norm_acc, pair_send, pair_recv, norm_send, norm_recv,
-     core_send, core_recv, chip_send, chip_recv,
+     core_send, core_recv, chip_send, chip_recv, top_send, top_recv, total_acc,
      eig_sem, pair_ssem, pair_rsem, norm_ssem, norm_rsem,
      core_ssem, core_rsem, chip_ssem, chip_rsem, small_sem) = refs[15:]
     rows, width = eig_buf.shape
     block = rows // n
+    piece = block // PARTS
     slab = shifts.shape[1]
     pairs = src.shape[2]
     tiles, lists = width // LANES, pairs // LANES
@@ -152,50 +155,67 @@
     for load in loads:
         load.wait()
 
-    def product(owner):
-        left = eig_buf[pl.ds(pl.multiple_of(owner * block, block), block), :]
+    def product(owner, part):
+        first = pl.multiple_of(owner * block + part * piece, piece)
+        left = eig_buf[pl.ds(first, piece), :]
         dims = (((1,), (1,)), ((), ()))
         return (lax.dot_general(left, slab_hi[...], dims, preferred_element_type=jnp.float32)
                 + lax.dot_general(left, slab_lo[...], dims, preferred_element_type=jnp.float32))
 
-    core_copies, chip_copies = [], []
-
-    def to_core(step, owner_chip):
-        core_send[step] = product(owner_chip * 2 + other)
+    core_copies, chip_copies = {}, {}
+
+    def to_core(step, part, owner_chip):
+        core_send[step, part] = product(owner_chip * 2 + other, part)
         copy = pltpu.make_async_remote_copy(
-            src_ref=core_send.at[step], dst_ref=core_recv.at[step], send_sem=core_ssem.at[step],
-            recv_sem=core_rsem.at[step], device_id=col(chip * 2 + other), device_id_type=MESH)
+            src_ref=core_send.at[step, part], dst_ref=core_recv.at[step, part],
+            send_sem=core_ssem.at[step, part], recv_sem=core_rsem.at[step, part],
+            device_id=col(chip * 2 + other), device_id_type=MESH)
         copy.start()
-        core_copies.append(copy)
+        core_copies[step, part] = copy
+
+    def to_chip(step, part, away):
+        copies = []
+        for at, (source, target) in enumerate(((chip_send, chip_recv), (top_send, top_recv))):
+            copy = pltpu.make_async_remote_copy(
+                src_ref=source.at[step, part], dst_ref=target.at[step, part],
+                send_sem=chip_ssem.at[at, step, part], recv_sem=chip_rsem.at[at, step, part],
+                device_id=col(away * 2 + core), device_id_type=MESH)
+            copy.start()
+            copies.append(copy)
+        chip_copies[step, part] = copies
 
     for step in range(1, chips):
         away = lax.rem(chip + step, chips)
-        to_core(step, away)
-        mine = product(away * 2 + core)
-        core_copies[-1].wait_recv()
-        chip_send[step] = mine + core_recv[step]
-        copy = pltpu.make_async_remote_copy(
-            src_ref=chip_send.at[step], dst_ref=chip_recv.at[step], send_sem=chip_ssem.at[step],
-            recv_sem=chip_rsem.at[step], device_id=col(away * 2 + core), device_id_type=MESH)
-        copy.start()
-        chip_copies.append(copy)
-    to_core(0, chip)
-    total = product(me)
-    core_copies[-1].wait_recv()
-    chip_send[0] = total + core_recv[0]
+        for part in range(PARTS):
+            to_core(step, part, away)
+        for part in range(PARTS):
+            mine = product(away * 2 + core, part)
+            core_copies[step, part].wait_recv()
+            mine = mine + core_recv[step, part]
+            top = jnp.maximum(jnp.max(jnp.abs(mine), axis=0, keepdims=True), 1e-33)
+            chip_send[step, part] = jnp.round(mine * (STEPS / top)).astype(jnp.int32).astype(jnp.int16)
+            top_send[step, part] = jnp.broadcast_to(top, top_send.shape[2:])
+            to_chip(step, part, away)
+    for part in range(PARTS):
+        to_core(0, part, chip)
+    for part in range(PARTS):
+        total_acc[part] = product(me, part)
 
     normsq = norm_send[0:1, :]
     for step, copy in enumerate(norm_copies):
         copy.wait()
         normsq = normsq + norm_recv[step + 1, 0:1, :]
     scale = jnp.sqrt(normsq)
-    for copy in chip_copies:
-        copy.wait()
-    total = chip_send[0]
-    for step in range(1, chips):
-        total = total + chip_recv[step]
-    out[...] = (total / scale).astype(out.dtype)
-    for copy in core_copies:
+    for part in range(PARTS):
+        core_copies[0, part].wait_recv()
+        total = total_acc[part] + core_recv[0, part]
+        for step in range(1, chips):
+            for copy in chip_copies[step, part]:
+                copy.wait()
+            unit = top_recv[step, part, 0:1, :] * (1.0 / STEPS)
+            total = total + chip_recv[step, part].astype(jnp.int32).astype(jnp.float32) * unit
+        out[part * piece:(part + 1) * piece, :] = (total / scale).astype(out.dtype)
+    for copy in core_copies.values():
         copy.wait_send()
 
 
@@ -205,6 +225,7 @@
     slab = small[2].shape[1]
     pairs = small[3].shape[2]
     block = rows // n
+    piece = block // PARTS
     chips = n // 2
     tiles = width // LANES
     f32, bf16 = jnp.float32, jnp.bfloat16
@@ -212,7 +233,7 @@
     dma = pltpu.SemaphoreType.DMA
     return pl.pallas_call(
         functools.partial(kernel, n),
-        out_shape=jax.ShapeDtypeStruct((block, slab), bf16),
+        out_shape=pltpu.VMEM((block, slab), bf16),
         in_specs=[pl.BlockSpec(memory_space=pltpu.HBM)] * 8,
         out_specs=vmem,
         scratch_shapes=[
@@ -234,12 +255,15 @@
             pltpu.VMEM((2, 8, LANES), f32),
             pltpu.VMEM((8, slab), f32),
             pltpu.VMEM((n, 8, slab), f32),
-            pltpu.VMEM((chips, block, slab), f32),
-            pltpu.VMEM((chips, block, slab), f32),
-            pltpu.VMEM((chips, block, slab), f32),
-            pltpu.VMEM((chips, block, slab), f32),
+            pltpu.VMEM((chips, PARTS, piece, slab), f32),
+            pltpu.VMEM((chips, PARTS, piece, slab), f32),
+            pltpu.VMEM((chips, PARTS, piece, slab), jnp.int16),
+            pltpu.VMEM((chips, PARTS, piece, slab), jnp.int16),
+            pltpu.VMEM((chips, PARTS, 8, slab), f32),
+            pltpu.VMEM((chips, PARTS, 8, slab), f32),
+            pltpu.VMEM((PARTS, piece, slab), f32),
             dma((4,)), dma, dma, dma((n,)), dma((n,)),
-            dma((chips,)), dma((chips,)), dma((chips,)), dma((chips,)), dma((7,)),
+            dma((chips, PARTS)), dma((chips, PARTS)), dma((2, chips, PARTS)), dma((2, chips, PARTS)), dma((7,)),
         ],
         compiler_params=pltpu.CompilerParams(
             collective_id=0, has_side_effects=True, vmem_limit_bytes=60 * 2**20),

time: 19.7 us -> 17.1 us (0.87)
  Pallas kernels: 17.9 us -> 16.3 us
  local copies, waits for them, and re-layouts: 1.57 us -> 0.66 us
    pallas_call x1, Pallas kernels: 17.9 us -> 16.3 us  [body(): pl.pallas_call(functools.partial(kernel, n), out_shape=pltpu.VMEM((block,...]
    unnamed x1, local copies, waits for them, and re-layouts: 1.57 us -> 0.66 us
where the time goes in v4:
time: 17.1 us; the launch traced here: 16.9 us
  Pallas kernels  16.3 us (95%)
  local copies, waits for them, and re-layouts  0.66 us (4%)
    pallas_call x1, Pallas kernels, body(): pl.pallas_call(functools.partial(kernel, n), out_shape=pltpu.VMEM((block,...  16.3 us
    unnamed x1, local copies, waits for them, and re-layouts  0.66 us

profile of v4, /device:TPU:0, one launch (start us, length us, event | category | flops | bytes accessed | tf_op | source)
XLA Modules:
  0.0 16.9 jit_solution(13527299742970686713)
XLA Ops:
  0.0 16.3 %merge.1 = bf16[256,256]{1,0:T(8,128)(2,1)S(1)} custom-call(bf16[1,1024,2048]{2,1,0:T(8,128)(2,1)} %eig.1, f32[1,2048]{1,0:T(1,128)} %refs_0_.1, f32[1,2048]{1,0:T(1,128)} %refs_1_.1, f32[1,256]{1,0:T(1,128)} %refs_2_.1, s32[1,1,512]{2,1,0:T(1,128)} %refs_3_.1, s32[1,1,512]{2,1,0:T(1,128)} %refs_4_.1, f32[1,1,512]{2,1,0:T(1,128)} %refs_5_.1, ...), custom_call_target="tpu_custom_call" | custom-call | flops 2147483648 | bytes 4194304 | tf_op jit(solution)/shard_map/merge/pallas_call | solution.py:234
  16.3 0.7 %copy.10 = bf16[256,256]{1,0:T(8,128)(2,1)} copy(bf16[256,256]{1,0:T(8,128)(2,1)S(1)} %merge.1) | data formatting | bytes 262144

commit v5 on v4

--- a/solution.py
+++ b/solution.py
@@ -9,7 +9,7 @@
 
 LANES = 128
 SUB = 64
-PARTS = 2
+PARTS = 1
 STEPS = 32767.0
 MESH = pl.DeviceIdType.MESH
 
@@ -33,7 +33,7 @@
     poles, weights, shifts, src, dst, cosines, sines = small
     (eig_buf, slab_own, slab_hi, slab_lo, shift_t, src_t, dst_t, cos_t, listed, inv,
      part_b, part_q, norm_acc, pair_send, pair_recv, norm_send, norm_recv,
-     core_send, core_recv, chip_send, chip_recv, top_send, top_recv, total_acc,
+     core_send, core_recv, chip_send, chip_recv, top_send, top_recv, both_acc,
      eig_sem, pair_ssem, pair_rsem, norm_ssem, norm_rsem,
      core_ssem, core_rsem, chip_ssem, chip_rsem, small_sem) = refs[15:]
     rows, width = eig_buf.shape
@@ -155,17 +155,16 @@
     for load in loads:
         load.wait()
 
-    def product(owner, part):
-        first = pl.multiple_of(owner * block + part * piece, piece)
-        left = eig_buf[pl.ds(first, piece), :]
+    def product(owner_chip):
+        first = pl.multiple_of(owner_chip * 2 * block, 2 * block)
+        left = eig_buf[pl.ds(first, 2 * block), :]
         dims = (((1,), (1,)), ((), ()))
         return (lax.dot_general(left, slab_hi[...], dims, preferred_element_type=jnp.float32)
                 + lax.dot_general(left, slab_lo[...], dims, preferred_element_type=jnp.float32))
 
     core_copies, chip_copies = {}, {}
 
-    def to_core(step, part, owner_chip):
-        core_send[step, part] = product(owner_chip * 2 + other, part)
+    def to_core(step, part):
         copy = pltpu.make_async_remote_copy(
             src_ref=core_send.at[step, part], dst_ref=core_recv.at[step, part],
             send_sem=core_ssem.at[step, part], recv_sem=core_rsem.at[step, part],
@@ -186,20 +185,21 @@
 
     for step in range(1, chips):
         away = lax.rem(chip + step, chips)
+        both_acc[...] = product(away).reshape(both_acc.shape)
+        core_send[step] = both_acc[other]
         for part in range(PARTS):
-            to_core(step, part, away)
+            to_core(step, part)
         for part in range(PARTS):
-            mine = product(away * 2 + core, part)
             core_copies[step, part].wait_recv()
-            mine = mine + core_recv[step, part]
+            mine = both_acc[core, part] + core_recv[step, part]
             top = jnp.maximum(jnp.max(jnp.abs(mine), axis=0, keepdims=True), 1e-33)
             chip_send[step, part] = jnp.round(mine * (STEPS / top)).astype(jnp.int32).astype(jnp.int16)
             top_send[step, part] = jnp.broadcast_to(top, top_send.shape[2:])
             to_chip(step, part, away)
+    both_acc[...] = product(chip).reshape(both_acc.shape)
+    core_send[0] = both_acc[other]
     for part in range(PARTS):
-        to_core(0, part, chip)
-    for part in range(PARTS):
-        total_acc[part] = product(me, part)
+        to_core(0, part)
 
     normsq = norm_send[0:1, :]
     for step, copy in enumerate(norm_copies):
@@ -208,7 +208,7 @@
     scale = jnp.sqrt(normsq)
     for part in range(PARTS):
         core_copies[0, part].wait_recv()
-        total = total_acc[part] + core_recv[0, part]
+        total = both_acc[core, part] + core_recv[0, part]
         for step in range(1, chips):
             for copy in chip_copies[step, part]:
                 copy.wait()
@@ -261,7 +261,7 @@
             pltpu.VMEM((chips, PARTS, piece, slab), jnp.int16),
             pltpu.VMEM((chips, PARTS, 8, slab), f32),
             pltpu.VMEM((chips, PARTS, 8, slab), f32),
-            pltpu.VMEM((PARTS, piece, slab), f32),
+            pltpu.VMEM((2, PARTS, piece, slab), f32),
             dma((4,)), dma, dma, dma((n,)), dma((n,)),
             dma((chips, PARTS)), dma((chips, PARTS)), dma((2, chips, PARTS)), dma((2, chips, PARTS)), dma((7,)),
         ],

time: 17.1 us -> 15.7 us (0.918)
  Pallas kernels: 16.3 us -> 14.8 us
    pallas_call x1, Pallas kernels: 16.3 us -> 14.8 us  [body(): pl.pallas_call(functools.partial(kernel, n), out_shape=pltpu.VMEM((block,...]
where the time goes in v5:
time: 15.7 us; the launch traced here: 15.5 us
  Pallas kernels  14.8 us (94%)
  local copies, waits for them, and re-layouts  0.66 us (4%)
    pallas_call x1, Pallas kernels, body(): pl.pallas_call(functools.partial(kernel, n), out_shape=pltpu.VMEM((block,...  14.8 us
    unnamed x1, local copies, waits for them, and re-layouts  0.66 us

profile of v5, /device:TPU:0, one launch (start us, length us, event | category | flops | bytes accessed | tf_op | source)
XLA Modules:
  0.0 15.5 jit_solution(14049312105476449504)
XLA Ops:
  0.0 14.8 %merge.1 = bf16[256,256]{1,0:T(8,128)(2,1)S(1)} custom-call(bf16[1,1024,2048]{2,1,0:T(8,128)(2,1)} %eig.1, f32[1,2048]{1,0:T(1,128)} %refs_0_.1, f32[1,2048]{1,0:T(1,128)} %refs_1_.1, f32[1,256]{1,0:T(1,128)} %refs_2_.1, s32[1,1,512]{2,1,0:T(1,128)} %refs_3_.1, s32[1,1,512]{2,1,0:T(1,128)} %refs_4_.1, f32[1,1,512]{2,1,0:T(1,128)} %refs_5_.1, ...), custom_call_target="tpu_custom_call" | custom-call | flops 2147483648 | bytes 4194304 | tf_op jit(solution)/shard_map/merge/pallas_call | solution.py:234
  14.8 0.7 %copy.10 = bf16[256,256]{1,0:T(8,128)(2,1)} copy(bf16[256,256]{1,0:T(8,128)(2,1)S(1)} %merge.1) | data formatting | bytes 262144

commit v6 on v5

--- a/solution.py
+++ b/solution.py
@@ -150,7 +150,7 @@
             slab_lo[r:r + SUB, cut] = (total - high.astype(jnp.float32)).astype(jnp.bfloat16)
         return carry
 
-    lax.fori_loop(0, tiles, partner_part, 0)
+    lax.fori_loop(0, tiles, partner_part, 0, unroll=4)
 
     for load in loads:
         load.wait()

time: 15.7 us -> 15.5 us (0.987)
  no operation moved by 1% of the time
where the time goes in v6:
time: 15.5 us; the launch traced here: 15.4 us
  Pallas kernels  14.7 us (95%)
  local copies, waits for them, and re-layouts  0.66 us (4%)
    pallas_call x1, Pallas kernels, body(): pl.pallas_call(functools.partial(kernel, n), out_shape=pltpu.VMEM((block,...  14.7 us
    unnamed x1, local copies, waits for them, and re-layouts  0.66 us

profile of v6, /device:TPU:0, one launch (start us, length us, event | category | flops | bytes accessed | tf_op | source)
XLA Modules:
  0.0 15.4 jit_solution(6626662436997588827)
XLA Ops:
  0.0 14.7 %merge.1 = bf16[256,256]{1,0:T(8,128)(2,1)S(1)} custom-call(bf16[1,1024,2048]{2,1,0:T(8,128)(2,1)} %eig.1, f32[1,2048]{1,0:T(1,128)} %refs_0_.1, f32[1,2048]{1,0:T(1,128)} %refs_1_.1, f32[1,256]{1,0:T(1,128)} %refs_2_.1, s32[1,1,512]{2,1,0:T(1,128)} %refs_3_.1, s32[1,1,512]{2,1,0:T(1,128)} %refs_4_.1, f32[1,1,512]{2,1,0:T(1,128)} %refs_5_.1, ...), custom_call_target="tpu_custom_call" | custom-call | flops 2147483648 | bytes 4194304 | tf_op jit(solution)/shard_map/merge/pallas_call | solution.py:234
  14.7 0.7 %copy.10 = bf16[256,256]{1,0:T(8,128)(2,1)} copy(bf16[256,256]{1,0:T(8,128)(2,1)S(1)} %merge.1) | data formatting | bytes 262144
